TPU v7x, 32 devices: a whole 2x2x4 slice. The times are simulated.
32 devices in a mesh: draw: 8 (over z, x), vocab: 4 (over y, core).
Axes of the slice: x: 2, y: 2, z: 4, core: 2. Of those that a mesh axis runs over, the one named last changes fastest.
Arguments:
- hidden: bfloat16 [16, 384, 896], P('draw'), may hold values from -256 to 256
- unembed: bfloat16 [896, 76032], P('draw', 'vocab'), may hold values from -1 to 1
- targets: int32 [384], replicated, may hold values from 0 to 76031
Outputs:
- influence: float32 [256, 128], P('draw')
All inputs are finite; a program needn't handle non-finite values.
Results may differ from a plain program's by a relative error of at most 0.0003.
Values may be sent and summed in bfloat16 or wider, within the bound.
A program may use at most 192 MiB of HBM per device.

v0:
```python
import jax
import jax.numpy as jnp
from jax import lax
from jax.sharding import PartitionSpec as P

TRAIN = 256


def swapped(x, axis, stride):
    return lax.ppermute(x, axis, [(i, i ^ 1 << stride) for i in range(lax.axis_size(axis))])


def merged(part, axis, combine):
    gathered = jax.tree.map(lambda a: lax.all_gather(a, axis), part)

    def take(source):
        return jax.tree.map(lambda a: lax.dynamic_index_in_dim(a, source, 0, False), gathered)

    return lax.fori_loop(
        1, lax.axis_size(axis), lambda source, state: combine(state, take(source)), take(0)
    )


def stats_of(logits, targets, first_column):
    row_max = jnp.max(logits, axis=1)
    row_total = jnp.sum(jnp.exp(logits - row_max[:, None]), axis=1)
    indices = first_column + lax.broadcasted_iota(jnp.int32, logits.shape, 1)
    chosen = jnp.sum(jnp.where(indices == targets[:, None], logits, 0.0), axis=1)
    return (row_max, row_total, chosen)


def combine_stats(left_stats, right_stats):
    joined = jnp.maximum(left_stats[0], right_stats[0])
    summed = left_stats[1] * jnp.exp(left_stats[0] - joined) + right_stats[1] * jnp.exp(
        right_stats[0] - joined
    )
    return (joined, summed, left_stats[2] + right_stats[2])


def covariance(train_losses, query_losses):
    train_centered = train_losses - jnp.mean(train_losses, axis=0, keepdims=True)
    query_centered = query_losses - jnp.mean(query_losses, axis=0, keepdims=True)
    draw_count = train_losses.shape[0]
    return jnp.dot(
        train_centered.T,
        query_centered,
        precision=lax.Precision.HIGHEST,
        preferred_element_type=jnp.float32,
    ) / (draw_count - 1.0)


def body(hidden, unembed, targets):
    per_device, tokens_each, model_width = hidden.shape
    draw_devices = lax.axis_size("draw")
    owned_count = TRAIN // draw_devices
    draw_index = lax.axis_index("draw")
    inner_index = draw_index % 4
    column_count = unembed.shape[1]
    quarter_count = column_count // 4
    repeated = jnp.tile(unembed, (1, draw_devices // 4))
    columns = lax.all_to_all(repeated, "draw", split_axis=1, concat_axis=0, tiled=True)
    first_column = lax.axis_index("vocab") * column_count + inner_index * quarter_count
    group_rows = hidden
    for bit_number in (0, 1):
        partner = swapped(group_rows, "draw", bit_number)
        lower_first = jnp.concatenate([group_rows, partner], axis=0)
        upper_first = jnp.concatenate([partner, group_rows], axis=0)
        group_rows = jnp.where(draw_index // 2**bit_number % 2 == 0, lower_first, upper_first)
    group_draws = group_rows.shape[0]
    logits = jnp.dot(
        group_rows.reshape(group_draws * tokens_each, model_width),
        columns,
        preferred_element_type=jnp.float32,
    )
    fresh_stats = stats_of(logits, jnp.tile(targets, group_draws), first_column)
    total_draws = per_device * draw_devices
    group_start = draw_index // 4 * group_draws
    blank_max = jnp.full((total_draws, tokens_each), -1e30, jnp.float32)
    blank_zero = jnp.zeros((total_draws, tokens_each), jnp.float32)
    local_stats = tuple(
        (
            lax.dynamic_update_slice_in_dim(
                blank_table, fresh.reshape(group_draws, tokens_each), group_start, 0
            )
            for blank_table, fresh in zip((blank_max, blank_zero, blank_zero), fresh_stats)
        )
    )
    row_max, row_total, chosen = merged(local_stats, ("draw", "vocab"), combine_stats)
    losses = row_max + jnp.log(row_total) - chosen
    train_losses = lax.dynamic_slice_in_dim(
        losses[:, :TRAIN], draw_index * owned_count, owned_count, 1
    )
    query_losses = losses[:, TRAIN:]
    return covariance(train_losses, query_losses)


def solution(mesh):
    placed = (P("draw", None, None), P("draw", "vocab"), P())
    return jax.shard_map(
        body, mesh=mesh, in_specs=placed, out_specs=P("draw", None), check_vma=False
    )
```

profile of v0, /device:TPU:0, one launch (start us, length us, event | category | flops | bytes accessed | tf_op | source)
XLA Modules:
  0.0 470.2 jit_solution(18411575401141903756)
XLA Ops:
  0.0 9.3 %tile.4 = bf16[112,2,19008]{2,1,0:T(2,128)(2,1)} broadcast(bf16[112,19008]{1,0:T(8,128)(2,1)} %param.6), dimensions={0,2} | broadcast | bytes 12773376 | tf_op jit(solution)/shard_map/tile | solution.py:60
  9.3 22.4 %all_to_all.14 = bf16[112,8,4752]{2,1,0:T(8,128)(2,1)} reshape(bf16[112,2,19008]{2,1,0:T(2,128)(2,1)} %tile.4) | data formatting | bytes 17031168 | tf_op jit(solution)/shard_map/all_to_all | solution.py:61
  31.7 8.3 %copy.5 = bf16[112,8,4752]{2,0,1:T(8,128)(2,1)} copy(bf16[112,8,4752]{2,1,0:T(8,128)(2,1)} %all_to_all.14) | data formatting | bytes 17031168 | tf_op jit(solution)/shard_map/all_to_all | solution.py:61
  40.0 0.0 copy-start
  40.0 7.4 %all-to-all-start = ((bf16[112,8,4752]{2,0,1:T(8,128)(2,1)}), bf16[112,8,4752]{2,0,1:T(8,128)(2,1)}, u32[]{:S(2)}, u32[]{:S(2)}) async-start(bf16[112,8,4752]{2,0,1:T(8,128)(2,1)} %copy.5), calls=%async_computation | async-start | bytes 17432576 | tf_op jit(solution)/shard_map/all_to_all | solution.py:61
  47.4 0.0 copy-done
  47.4 0.0 copy-start.1
  47.4 2.1 collective-permute-start
  49.5 123.2 %collective-permute-done = bf16[2,384,896]{2,1,0:T(8,128)(2,1)} collective-permute-done((bf16[2,384,896]{2,1,0:T(8,128)(2,1)S(1)}, bf16[2,384,896]{2,1,0:T(8,128)(2,1)}, u32[]{:S(2)}, u32[]{:S(2)}) %collective-permute-start) | collective-permute-done | bytes 1376288 | tf_op jit(solution)/shard_map/ppermute | solution.py:10
  172.7 3.0 maximum_select_fusion.1
  175.7 0.1 collective-permute-start.1
  175.9 0.0 copy-done.1
  175.9 105.6 %collective-permute-done.1 = bf16[4,384,896]{2,1,0:T(8,128)(2,1)} collective-permute-done((bf16[4,384,896]{2,1,0:T(8,128)(2,1)S(1)}, bf16[4,384,896]{2,1,0:T(8,128)(2,1)}, u32[]{:S(2)}, u32[]{:S(2)}) %collective-permute-start.1) | collective-permute-done | bytes 2752544 | tf_op jit(solution)/shard_map/ppermute | solution.py:10
  281.6 6.3 %maximum_select_fusion = bf16[8,384,896]{2,1,0:T(8,128)(2,1)} fusion(bf16[4,384,896]{2,1,0:T(8,128)(2,1)} %collective-permute-done.1, bf16[4,384,896]{2,1,0:T(8,128)(2,1)S(1)} %maximum_select_fusion.1, pred[]{:T(512)S(6)} %eq.20), kind=kLoop, calls=%fused_computation.8 | loop fusion | flops 8257536 | bytes 11010049 | tf_op jit(solution)/shard_map/jit(_where)/select_n | solution.py:68
  287.8 0.0 all-to-all-done
  287.8 39.3 %fusion.9 = (f32[3072]{0:T(1024)S(1)}, f32[3072,4752]{0,1:T(8,128)}) fusion(bf16[3072,896]{1,0:T(8,128)(2,1)} %bitcast.28, bf16[896,4752]{1,0:T(8,128)(2,1)} %bitcast.5), kind=kOutput, calls=%fused_computation.30 | convolution fusion | flops 26174468096 | bytes 72425472 | tf_op jit(solution)/shard_map/dot_general | solution.py:70
  327.1 20.0 %select_reduce_fusion = (f32[3072]{0:T(1024)S(1)}, f32[3072]{0:T(1024)S(1)}) fusion(f32[3072,4752]{0,1:T(8,128)} %get-tuple-element.206, s32[3072]{0:T(1024)S(1)} %eq.22, s32[4752]{0:T(1024)S(1)} %iota_add_fusion, f32[3072]{0:T(1024)S(1)} %get-tuple-element.205), kind=kLoop, calls=%fused_computation.6 | loop fusion | flops 72984576 | bytes 58460736 | tf_op jit(solution)/shard_map/reduce_sum | solution.py:28
  347.2 41.3 %all_gather.23 = f32[32,16,384]{2,1,0:T(8,128)S(1)} all-gather(f32[1,16,384]{2,1,0:T(8,128)S(1)} %constant_dynamic-update-slice_fusion), channel_id=1, replica_groups=mesh['draw'=8,'vocab'=4] {'draw','vocab'}, dimensions={0}, use_global_device_ids=true | all-gather | bytes 811008 | tf_op jit(solution)/shard_map/all_gather | solution.py:14
  388.5 38.8 %all_gather.21 = f32[32,16,384]{2,1,0:T(8,128)S(1)} all-gather(f32[1,16,384]{2,1,0:T(8,128)S(1)} %constant_dynamic-update-slice_fusion.1), channel_id=1, replica_groups=mesh['draw'=8,'vocab'=4] {'draw','vocab'}, dimensions={0}, use_global_device_ids=true | all-gather | bytes 811008 | tf_op jit(solution)/shard_map/all_gather | solution.py:14
  427.3 40.2 %all_gather.19 = f32[32,16,384]{2,1,0:T(8,128)S(1)} all-gather(f32[1,16,384]{2,1,0:T(8,128)S(1)} %constant_dynamic-update-slice_fusion.2), channel_id=1, replica_groups=mesh['draw'=8,'vocab'=4] {'draw','vocab'}, dimensions={0}, use_global_device_ids=true | all-gather | bytes 811008 | tf_op jit(solution)/shard_map/all_gather | solution.py:14
  467.5 1.7 while.19
  469.2 0.1 dynamic-slice_reduce_fusion
  469.3 0.9 convolution_multiply_fusion
  (51 shorter events, 1.0 us)
Async XLA Ops:
  40.0 7.4 %copy-start = (bf16[2,384,896]{2,1,0:T(8,128)(2,1)S(1)}, bf16[2,384,896]{2,1,0:T(8,128)(2,1)}, u32[]{:S(2)}) copy-start(bf16[2,384,896]{2,1,0:T(8,128)(2,1)} %param.5) | copy-start | bytes 4128772
  40.0 247.8 %all-to-all-start = ((bf16[112,8,4752]{2,0,1:T(8,128)(2,1)}), bf16[112,8,4752]{2,0,1:T(8,128)(2,1)}, u32[]{:S(2)}, u32[]{:S(2)}) async-start(bf16[112,8,4752]{2,0,1:T(8,128)(2,1)} %copy.5), calls=%async_computation | async-start | bytes 17432576 | tf_op jit(solution)/shard_map/all_to_all | solution.py:61
  47.4 128.4 %copy-start.1 = (s32[384]{0:T(512)S(1)}, s32[384]{0:T(512)}, u32[]{:S(2)}) copy-start(s32[384]{0:T(512)} %param.7) | copy-start | bytes 4612
  47.4 125.3 %collective-permute-start = (bf16[2,384,896]{2,1,0:T(8,128)(2,1)S(1)}, bf16[2,384,896]{2,1,0:T(8,128)(2,1)}, u32[]{:S(2)}, u32[]{:S(2)}) collective-permute-start(bf16[2,384,896]{2,1,0:T(8,128)(2,1)S(1)} %copy-done), channel_id=1, source_target_pairs={{0,4},{4,0},{8,12},{12,8},{16,20},{20,16},{24,28},{28,24},{1,5},{5... | collective-permute-start | bytes 4128776 | tf_op jit(solution)/shard_map/ppermute | solution.py:10
  175.7 105.8 %collective-permute-start.1 = (bf16[4,384,896]{2,1,0:T(8,128)(2,1)S(1)}, bf16[4,384,896]{2,1,0:T(8,128)(2,1)}, u32[]{:S(2)}, u32[]{:S(2)}) collective-permute-start(bf16[4,384,896]{2,1,0:T(8,128)(2,1)S(1)} %maximum_select_fusion.1), channel_id=1, source_target_pairs={{0,8},{4,12},{8,0},{12,4},{16,24},{20,28},{24,16},{28,20},{1,9},{5... | collective-permute-start | bytes 8257544 | tf_op jit(solution)/shard_map/ppermute | solution.py:10
where the time goes:
time: 471 us; the launch traced here: 470 us
  waiting for transfers between devices  229 us (49%)
  blocking collectives  120 us (25%)
  matrix products  40.2 us (9%)
  local copies, waits for them, and re-layouts  40.1 us (9%)
  other arithmetic  30.3 us (6%)
  starting transfers between devices  9.55 us (2%)
    ppermute x2, waiting for transfers between devices, swapped(): lax.ppermute(x, axis, [(i, i ^ 1 << stride) for i in range(lax.axis_size(...  229 us
    all_gather x3, blocking collectives, merged(): gathered = jax.tree.map(lambda a: lax.all_gather(a, axis), part)  120 us
    dot_general x1, matrix products, body(): jnp.dot(group_rows.reshape(group_draws * tokens_each, model_width), colum...  39.3 us
    all_to_all x2, local copies, waits for them, and re-layouts, body(): lax.all_to_all(repeated, 'draw', split_axis=1, concat_axis=0, tiled=True)  30.7 us
    reduce_sum x1, other arithmetic, stats_of(): jnp.sum(jnp.where(indices == targets[:, None], logits, 0.0), axis=1)  20 us
  transfers between devices with their start and end apart: 3, of which 2 were waited for; matrix products, arithmetic and copies ran while one was open for 2% of the time, Pallas kernels for 0%

commit v1 on v0

--- a/solution.py
+++ b/solution.py
@@ -1,7 +1,18 @@
+import functools
+
 import jax
 import jax.numpy as jnp
 from jax import lax
+from jax.experimental import pallas as pl
+from jax.experimental.pallas import tpu as pltpu
 from jax.sharding import PartitionSpec as P
+
+MESH = pl.DeviceIdType.MESH
+LANES = 128
+GROUP = 32
+LOWEST = -1e30
+WIDEST = 5
+NARROW = 2
 
 TRAIN = 256
 
@@ -94,8 +105,483 @@
     return covariance(train_losses, query_losses)
 
 
+def chunk_plan(column_count, draw_devices):
+    full_tiles, rest = divmod(column_count, LANES)
+    tiles = full_tiles + (rest > 0)
+    share = -(-tiles // draw_devices)
+    last_full = full_tiles - (draw_devices - 1) * share
+    last_count = column_count - (draw_devices - 1) * share * LANES
+    return share, last_full, last_count, rest
+
+
+def cut(start, total, widest):
+    pieces = []
+    while total:
+        width = min(widest, total)
+        pieces.append((start * LANES, width * LANES))
+        start, total = start + width, total - width
+    return pieces
+
+
+def kernel(
+    plan,
+    chunks,
+    h_ref,
+    u_ref,
+    tail_ref,
+    t_ref,
+    out_ref,
+    hbuf,
+    w,
+    wt,
+    xbuf,
+    mst,
+    sst,
+    cst,
+    stat_out,
+    stat_in,
+    vocab_out,
+    vocab_in,
+    loss_out,
+    loss_in,
+    own_sem,
+    hsend,
+    hrecv,
+    usend,
+    urecv,
+    ssend,
+    srecv,
+    vsend,
+    vrecv,
+    lsend,
+    lrecv,
+):
+    nd, nv = lax.axis_size("draw"), lax.axis_size("vocab")
+    share, last_full, last_count, rest = plan
+    length = nd // 2
+    k, v = lax.axis_index("draw"), lax.axis_index("vocab")
+    line, side, core = k // 2, k % 2, v % 2
+    depth = u_ref.shape[0]
+    block = share * LANES
+    full_end = last_full * LANES
+    is_last = k == nd - 1
+    wide = t_ref.shape[1]
+
+    def draw_peer(j):
+        return lax.rem(k + j, nd)
+
+    def vocab_peer(j):
+        return lax.rem(v + j, nv)
+
+    def rows_of(source):
+        return pl.ds(pl.multiple_of(source * depth, 16), depth)
+
+    barrier = pltpu.get_barrier_semaphore()
+
+    @pl.loop(1, nd)
+    def _(j):
+        pl.semaphore_signal(barrier, inc=1, device_id=(draw_peer(j), v), device_id_type=MESH)
+
+    @pl.loop(1, nv)
+    def _(j):
+        pl.semaphore_signal(barrier, inc=1, device_id=(k, vocab_peer(j)), device_id_type=MESH)
+
+    pl.semaphore_wait(barrier, nd + nv - 2)
+
+    def hidden_copy(source, where, own=False):
+        slot = 2 * source + core
+        target = [
+            (jnp.minimum(k + 2, nd - 1), v),
+            (jnp.maximum(k - 2, 0), v),
+            (k + 1 - 2 * side, v),
+            (k, v + 1 - 2 * core),
+        ][where]
+        return pltpu.make_async_remote_copy(
+            src_ref=h_ref.at[core] if own else hbuf.at[slot],
+            dst_ref=hbuf.at[slot],
+            send_sem=hsend.at[source, where],
+            recv_sem=hrecv.at[slot],
+            device_id=target,
+            device_id_type=MESH,
+        )
+
+    def hidden_wait(slot):
+        pltpu.make_async_copy(h_ref.at[0], hbuf.at[slot], hrecv.at[slot]).wait()
+
+    can_up, can_down = line + 1 < length, line > 0
+
+    @pl.when(can_up)
+    def _():
+        hidden_copy(k, 0, own=True).start()
+
+    @pl.when(can_down)
+    def _():
+        hidden_copy(k, 1, own=True).start()
+
+    hidden_copy(k, 2, own=True).start()
+    own_hidden = [
+        pltpu.make_async_copy(h_ref.at[i], hbuf.at[2 * k + i], own_sem.at[i]) for i in range(2)
+    ]
+    for copy in own_hidden:
+        copy.start()
+
+    def pieces_of(chunk, last):
+        start, width = chunks[chunk]
+        if not last or start + width <= full_end:
+            return [(u_ref, None, start, width)]
+        return [(tail_ref, 0, start, LANES)] if rest and start == full_end else []
+
+    def columns_copy(chunk, target, piece):
+        ref, fixed, start, width = piece
+        first = pl.multiple_of(target * block + start, LANES) if fixed is None else fixed
+        return ref.at[:, pl.ds(first, width)], w.at[rows_of(k), pl.ds(start, width)]
+
+    def for_target(chunk, target, act):
+        @pl.when(target < nd - 1)
+        def _():
+            for piece in pieces_of(chunk, False):
+                act(piece)
+
+        @pl.when(target == nd - 1)
+        def _():
+            for piece in pieces_of(chunk, True):
+                act(piece)
+
+    def remote_columns(chunk, target, piece):
+        source_ref, target_ref = columns_copy(chunk, target, piece)
+        return pltpu.make_async_remote_copy(
+            src_ref=source_ref,
+            dst_ref=target_ref,
+            send_sem=usend.at[chunk, target],
+            recv_sem=urecv.at[chunk, k],
+            device_id=(target, v),
+            device_id_type=MESH,
+        )
+
+    def local_columns(chunk, piece):
+        source_ref, target_ref = columns_copy(chunk, k, piece)
+        return pltpu.make_async_copy(source_ref, target_ref, urecv.at[chunk, k])
+
+    for chunk in range(len(chunks)):
+
+        @pl.loop(1, nd)
+        def _(j):
+            target = draw_peer(j)
+            for_target(chunk, target, lambda piece: remote_columns(chunk, target, piece).start())
+
+        for_target(chunk, k, lambda piece: local_columns(chunk, piece).start())
+
+    def across(source):
+        hidden_wait(2 * source + core)
+        hidden_copy(source, 3).start()
+
+    across(k + 1 - 2 * side)
+
+    @pl.loop(1, length)
+    def _(step):
+        @pl.when(line - step >= 0)
+        def _():
+            source = k - 2 * step
+            hidden_wait(2 * source + core)
+
+            @pl.when(can_up)
+            def _():
+                hidden_copy(source, 0).start()
+
+            hidden_copy(source, 2).start()
+            hidden_copy(source, 3).start()
+
+        @pl.when(line + step < length)
+        def _():
+            source = k + 2 * step
+            hidden_wait(2 * source + core)
+
+            @pl.when(can_down)
+            def _():
+                hidden_copy(source, 1).start()
+
+            hidden_copy(source, 2).start()
+            hidden_copy(source, 3).start()
+
+        @pl.when(line - step >= 0)
+        def _():
+            across(k - 2 * step + 1 - 2 * side)
+
+        @pl.when(line + step < length)
+        def _():
+            across(k + 2 * step + 1 - 2 * side)
+
+    for copy in own_hidden:
+        copy.wait()
+
+    @pl.loop(1, nd)
+    def _(j):
+        hidden_wait(2 * draw_peer(j) + 1 - core)
+
+    mst[...] = jnp.full_like(mst, LOWEST)
+    sst[...] = jnp.zeros_like(sst)
+    cst[...] = jnp.zeros_like(cst)
+
+    limit = jnp.where(is_last, last_count, block)
+    first_column = v * u_ref.shape[1] + k * block
+    relative = t_ref[...] - first_column
+    relative = jnp.where((relative >= 0) & (relative < limit), relative, -block)
+    relative = jnp.broadcast_to(relative, (8, wide)) - lax.broadcasted_iota(
+        jnp.int32, (8, wide), 0
+    )
+
+    for chunk, (start, width) in enumerate(chunks):
+
+        @pl.loop(0, nd)
+        def _(j):
+            source = draw_peer(j)
+
+            def arrived(piece):
+                _, _, first, count = piece
+                target_ref = w.at[rows_of(source), pl.ds(first, count)]
+                pltpu.make_async_copy(
+                    u_ref.at[:, pl.ds(0, count)], target_ref, urecv.at[chunk, source]
+                ).wait()
+
+            for_target(chunk, k, arrived)
+
+        groups = jnp.clip(limit - start, 0, width) // GROUP
+        wt[0:width, :] = w[:, start : start + width].T
+
+        @pl.loop(0, nd)
+        def _(pair):
+            rows = hbuf[pl.ds(2 * pair, 2)].reshape(wide, hbuf.shape[2])
+            xbuf[0:width, :] = lax.dot_general(
+                wt[0:width, :], rows, (((1,), (1,)), ((), ())), preferred_element_type=jnp.float32
+            )
+            old = mst[pair]
+
+            def largest(group, found):
+                for r in range(GROUP // 8):
+                    at = pl.multiple_of(group * GROUP + r * 8, 8)
+                    found = jnp.maximum(found, xbuf[pl.ds(at, 8), :])
+                return found
+
+            new = lax.fori_loop(0, groups, largest, old)
+
+            def totals(group, state):
+                total, chosen = state
+                for r in range(GROUP // 8):
+                    at = pl.multiple_of(group * GROUP + r * 8, 8)
+                    x = xbuf[pl.ds(at, 8), :]
+                    total = total + jnp.exp(x - new)
+                    chosen = chosen + jnp.where(relative == start + at, x, 0.0)
+                return total, chosen
+
+            total, chosen = lax.fori_loop(
+                0, groups, totals, (sst[pair] * jnp.exp(old - new), cst[pair])
+            )
+            mst[pair] = new
+            sst[pair] = total
+            cst[pair] = chosen
+
+    @pl.loop(0, nd)
+    def _(pair):
+        old = mst[pair]
+        top = jnp.max(old, axis=0, keepdims=True)
+        stat_out[pair] = jnp.zeros(stat_out.shape[1:], jnp.float32)
+        stat_out[pair, 0:1, :] = top
+        stat_out[pair, 1:2, :] = jnp.sum(sst[pair] * jnp.exp(old - top), axis=0, keepdims=True)
+        stat_out[pair, 2:3, :] = jnp.sum(cst[pair], axis=0, keepdims=True)
+
+    def stat_copy(target):
+        return pltpu.make_async_remote_copy(
+            src_ref=stat_out.at[target],
+            dst_ref=stat_in.at[k],
+            send_sem=ssend.at[target],
+            recv_sem=srecv.at[k],
+            device_id=(target, v),
+            device_id_type=MESH,
+        )
+
+    @pl.loop(1, nd)
+    def _(j):
+        stat_copy(draw_peer(j)).start()
+
+    def joined(state, part):
+        top = jnp.maximum(state[0], part[0:1])
+        total = state[1] * jnp.exp(state[0] - top) + part[1:2] * jnp.exp(part[0:1] - top)
+        return top, total, state[2] + part[2:3]
+
+    mine = stat_out[k]
+
+    def take_draw(j, state):
+        source = draw_peer(j)
+        pltpu.make_async_copy(stat_out.at[0], stat_in.at[source], srecv.at[source]).wait()
+        return joined(state, stat_in[source])
+
+    state = lax.fori_loop(1, nd, take_draw, (mine[0:1], mine[1:2], mine[2:3]))
+    vocab_out[...] = jnp.zeros_like(vocab_out)
+    for i in range(3):
+        vocab_out[i : i + 1, :] = state[i]
+
+    def vocab_copy(target):
+        return pltpu.make_async_remote_copy(
+            src_ref=vocab_out,
+            dst_ref=vocab_in.at[v],
+            send_sem=vsend.at[target],
+            recv_sem=vrecv.at[v],
+            device_id=(k, target),
+            device_id_type=MESH,
+        )
+
+    @pl.loop(1, nv)
+    def _(j):
+        vocab_copy(vocab_peer(j)).start()
+
+    vocab_in[v] = vocab_out[...]
+
+    @pl.loop(1, nv)
+    def _(j):
+        source = vocab_peer(j)
+        pltpu.make_async_copy(vocab_out, vocab_in.at[source], vrecv.at[source]).wait()
+
+    def take_vocab(source, state):
+        return joined(state, vocab_in[source])
+
+    first = vocab_in[0]
+    top, total, chosen = lax.fori_loop(1, nv, take_vocab, (first[0:1], first[1:2], first[2:3]))
+    loss_out[...] = jnp.broadcast_to(top + jnp.log(total) - chosen, loss_out.shape)
+
+    def loss_copy(target):
+        return pltpu.make_async_remote_copy(
+            src_ref=loss_out,
+            dst_ref=loss_in.at[k],
+            send_sem=lsend.at[target],
+            recv_sem=lrecv.at[k],
+            device_id=(target, v),
+            device_id_type=MESH,
+        )
+
+    @pl.loop(1, nd)
+    def _(j):
+        loss_copy(draw_peer(j)).start()
+
+    loss_in[k] = loss_out[...]
+
+    @pl.loop(1, nd)
+    def _(j):
+        source = draw_peer(j)
+        pltpu.make_async_copy(loss_out, loss_in.at[source], lrecv.at[source]).wait()
+
+    for source in range(nd):
+        out_ref[source : source + 1, :] = loss_in[source, 0:1, :]
+
+    @pl.loop(1, nd)
+    def _(j):
+        target = draw_peer(j)
+        for chunk in range(len(chunks)):
+            for_target(
+                chunk, target, lambda piece: remote_columns(chunk, target, piece).wait_send()
+            )
+        stat_copy(target).wait_send()
+        loss_copy(target).wait_send()
+        hidden_copy(target, 3).wait_send()
+
+    @pl.loop(1, nv)
+    def _(j):
+        vocab_copy(vocab_peer(j)).wait_send()
+
+    @pl.loop(0, length)
+    def _(place):
+        source = 2 * place + side
+
+        @pl.when((place <= line) & can_up)
+        def _():
+            hidden_copy(source, 0).wait_send()
+
+        @pl.when((place >= line) & can_down)
+        def _():
+            hidden_copy(source, 1).wait_send()
+
+        hidden_copy(source, 2).wait_send()
+
+
+def fused(plan, hidden, unembed, targets):
+    per_device, tokens_each, model_width = hidden.shape
+    nd, nv = lax.axis_size("draw"), lax.axis_size("vocab")
+    depth, column_count = unembed.shape
+    share, last_full, _, rest = plan
+    chunks = cut(0, last_full, WIDEST) + cut(last_full, share - last_full, NARROW)
+    widest = max(width for _, width in chunks)
+    count = len(chunks)
+    wide = 2 * tokens_each
+    tail = jnp.pad(unembed[:, column_count - rest :], ((0, 0), (0, LANES - rest)))
+    f32, bf16, dma = jnp.float32, jnp.bfloat16, pltpu.SemaphoreType.DMA
+    anywhere = pl.BlockSpec(memory_space=pl.ANY)
+    inside = pl.BlockSpec(memory_space=pltpu.VMEM)
+    losses = pl.pallas_call(
+        functools.partial(kernel, plan, chunks),
+        out_shape=jax.ShapeDtypeStruct((nd, wide), f32),
+        in_specs=[anywhere, anywhere, anywhere, inside],
+        out_specs=inside,
+        scratch_shapes=[
+            pltpu.VMEM((2 * nd, tokens_each, model_width), bf16),
+            pltpu.VMEM((model_width, share * LANES), bf16),
+            pltpu.VMEM((widest, model_width), bf16),
+            pltpu.VMEM((widest, wide), f32),
+            pltpu.VMEM((nd, 8, wide), f32),
+            pltpu.VMEM((nd, 8, wide), f32),
+            pltpu.VMEM((nd, 8, wide), f32),
+            pltpu.VMEM((nd, 8, wide), f32),
+            pltpu.VMEM((nd, 8, wide), f32),
+            pltpu.VMEM((8, wide), f32),
+            pltpu.VMEM((nv, 8, wide), f32),
+            pltpu.VMEM((8, wide), f32),
+            pltpu.VMEM((nd, 8, wide), f32),
+            dma((2,)),
+            dma((nd, 4)),
+            dma((2 * nd,)),
+            dma((count, nd)),
+            dma((count, nd)),
+            dma((nd,)),
+            dma((nd,)),
+            dma((nv,)),
+            dma((nv,)),
+            dma((nd,)),
+            dma((nd,)),
+        ],
+        compiler_params=pltpu.CompilerParams(
+            collective_id=0, has_side_effects=True, vmem_limit_bytes=48 * 1024 * 1024
+        ),
+    )(hidden, unembed, tail, jnp.tile(targets, 2)[None, :])
+    losses = losses.reshape(2 * nd, tokens_each)
+    owned_count = TRAIN // nd
+    train_losses = lax.dynamic_slice_in_dim(
+        losses[:, :TRAIN], lax.axis_index("draw") * owned_count, owned_count, 1
+    )
+    return covariance(train_losses, losses[:, TRAIN:])
+
+
+def placed_body(hidden, unembed, targets):
+    per_device, tokens_each, model_width = hidden.shape
+    nd, nv = lax.axis_size("draw"), lax.axis_size("vocab")
+    depth, column_count = unembed.shape
+    plan = chunk_plan(column_count, nd)
+    share, last_full, last_count, rest = plan
+    fits = (
+        per_device == 2
+        and nd % 2 == 0
+        and nv % 2 == 0
+        and depth % 16 == 0
+        and tokens_each % LANES == 0
+        and rest > 0
+        and rest % GROUP == 0
+        and 0 < last_full < share
+        and nd * 2 * tokens_each * model_width * 2 < 16 * 1024 * 1024
+    )
+    if fits:
+        return fused(plan, hidden, unembed, targets)
+    return body(hidden, unembed, targets)
+
+
 def solution(mesh):
     placed = (P("draw", None, None), P("draw", "vocab"), P())
     return jax.shard_map(
-        body, mesh=mesh, in_specs=placed, out_specs=P("draw", None), check_vma=False
-    )
+        placed_body, mesh=mesh, in_specs=placed, out_specs=P("draw", None), check_vma=False
+    )

time: 471 us -> 247 us (0.52)
  Pallas kernels: 0 us -> 241 us
  waiting for transfers between devices: 229 us -> 0 us
  blocking collectives: 120 us -> 0 us
  matrix products: 40.2 us -> 0.9 us
  local copies, waits for them, and re-layouts: 40.1 us -> 4.34 us
  other arithmetic: 30.3 us -> 0.12 us
  starting transfers between devices: 9.55 us -> 0 us
    pallas_call x0 -> x1, Pallas kernels: none -> 241 us  [fused(): pl.pallas_call(functools.partial(kernel, plan, chunks), out_shape=jax.Sha...]
    ppermute x2 -> x0, waiting for transfers between devices: 229 us -> none  [swapped(): lax.ppermute(x, axis, [(i, i ^ 1 << stride) for i in range(lax.axis_size(...]
    all_gather x3 -> x0, blocking collectives: 120 us -> none  [merged(): gathered = jax.tree.map(lambda a: lax.all_gather(a, axis), part)]
    dot_general x1 -> x0, matrix products: 39.3 us -> none  [body(): jnp.dot(group_rows.reshape(group_draws * tokens_each, model_width), colum...]
    all_to_all x2 -> x0, local copies, waits for them, and re-layouts: 30.7 us -> none  [body(): lax.all_to_all(repeated, 'draw', split_axis=1, concat_axis=0, tiled=True)]
    reduce_sum x1 -> x0, other arithmetic: 20 us -> none  [stats_of(): jnp.sum(jnp.where(indices == targets[:, None], logits, 0.0), axis=1)]
    another operation x2 -> x0, local copies, waits for them, and re-layouts: 9.26 us -> none  [the longest x1 9.26 us: body(): repeated = jnp.tile(unembed, (1, draw_devices // 4))]
    select_n x2 -> x0, other arithmetic: 9.24 us -> none  [body(): jnp.where(draw_index // 2 ** bit_number % 2 == 0, lower_first, upper_first)]
  transfers between devices with their start and end apart: 3 -> 0, of which waited for: 2 -> 0; matrix products, arithmetic and copies ran while one was open for 2% -> 0% of each run, Pallas kernels for 0% -> 0%
where the time goes in v1:
time: 247 us
  Pallas kernels  241 us (98%)
  local copies, waits for them, and re-layouts  4.34 us (2%)
    pallas_call x1, Pallas kernels, fused(): pl.pallas_call(functools.partial(kernel, plan, chunks), out_shape=jax.Sha...  241 us

profile of v1, /device:TPU:0, one launch (start us, length us, event | category | flops | bytes accessed | tf_op | source)
XLA Modules:
  0.0 246.6 jit_solution(6003613874803008310)
XLA Ops:
  0.0 0.0 copy-start
  0.0 0.8 slice.9
  0.8 0.0 copy-done
  0.8 0.0 copy-start.1
  0.8 2.2 copy-done.1
  3.0 0.0 copy-start.2
  3.0 1.3 copy-done.2
  4.4 241.2 %shard_map.37 = f32[8,768]{1,0:T(8,128)S(1)} custom-call(bf16[2,384,896]{2,1,0:T(8,128)(2,1)S(1)} %copy-done.2, bf16[112,19008]{1,0:T(8,128)(2,1)S(1)} %copy-done.1, bf16[112,128]{1,0:T(8,128)(2,1)S(1)} %pad.4.tail_ref, s32[1,768]{1,0:T(1,128)S(1)} %bitcast.4), custom_call_target="tpu_custom_call" | custom-call | tf_op jit(solution)/shard_map/pallas_call | solution.py:518
  245.6 0.1 dynamic-slice_reduce_fusion
  245.8 0.9 convolution_multiply_fusion
  (8 shorter events, 0.1 us)
Async XLA Ops:
  0.0 0.8 copy-start
  0.8 2.2 copy-start.1
  3.0 1.3 copy-start.2

commit v2 on v1

--- a/solution.py
+++ b/solution.py
@@ -13,6 +13,9 @@
 LOWEST = -1e30
 WIDEST = 5
 NARROW = 2
+FINE = 2
+FINE_CHUNKS = 2
+SEND_COUNTS = (1, 1, 1, 2, 2, 2)
 
 TRAIN = 256
 
@@ -123,9 +126,16 @@
     return pieces
 
 
+def unrolled(first, last, step, state):
+    for i in range(first, last):
+        state = step(i, state)
+    return state
+
+
 def kernel(
     plan,
     chunks,
+    sends,
     h_ref,
     u_ref,
     tail_ref,
@@ -135,6 +145,7 @@
     w,
     wt,
     xbuf,
+    xbuf_other,
     mst,
     sst,
     cst,
@@ -188,25 +199,38 @@
 
     pl.semaphore_wait(barrier, nd + nv - 2)
 
+    half = h_ref.shape[1] // 2
+
+    def part_of(ref, index, part):
+        return ref.at[index, pl.ds(pl.multiple_of(part // 2 * half, 16), half)]
+
     def hidden_copy(source, where, own=False):
-        slot = 2 * source + core
+        beside = v + 2 - 4 * (v // 2)
+        part = beside if where == 5 else v
+        place = part_of(hbuf, 2 * source + part % 2, part)
         target = [
             (jnp.minimum(k + 2, nd - 1), v),
             (jnp.maximum(k - 2, 0), v),
             (k + 1 - 2 * side, v),
+            (k, beside),
+            (k, v + 1 - 2 * core),
             (k, v + 1 - 2 * core),
         ][where]
         return pltpu.make_async_remote_copy(
-            src_ref=h_ref.at[core] if own else hbuf.at[slot],
-            dst_ref=hbuf.at[slot],
+            src_ref=part_of(h_ref, part % 2, part) if own else place,
+            dst_ref=place,
             send_sem=hsend.at[source, where],
-            recv_sem=hrecv.at[slot],
+            recv_sem=hrecv.at[source, part],
             device_id=target,
             device_id_type=MESH,
         )
 
-    def hidden_wait(slot):
-        pltpu.make_async_copy(h_ref.at[0], hbuf.at[slot], hrecv.at[slot]).wait()
+    def hidden_wait(source, part):
+        pltpu.make_async_copy(
+            part_of(h_ref, 0, part),
+            part_of(hbuf, 2 * source + part % 2, part),
+            hrecv.at[source, part],
+        ).wait()
 
     can_up, can_down = line + 1 < length, line > 0
 
@@ -226,7 +250,7 @@
         copy.start()
 
     def pieces_of(chunk, last):
-        start, width = chunks[chunk]
+        start, width = sends[chunk]
         if not last or start + width <= full_end:
             return [(u_ref, None, start, width)]
         return [(tail_ref, 0, start, LANES)] if rest and start == full_end else []
@@ -262,8 +286,7 @@
         source_ref, target_ref = columns_copy(chunk, k, piece)
         return pltpu.make_async_copy(source_ref, target_ref, urecv.at[chunk, k])
 
-    for chunk in range(len(chunks)):
-
+    def send_columns(chunk):
         @pl.loop(1, nd)
         def _(j):
             target = draw_peer(j)
@@ -271,52 +294,67 @@
 
         for_target(chunk, k, lambda piece: local_columns(chunk, piece).start())
 
-    def across(source):
-        hidden_wait(2 * source + core)
-        hidden_copy(source, 3).start()
-
-    across(k + 1 - 2 * side)
-
-    @pl.loop(1, length)
-    def _(step):
-        @pl.when(line - step >= 0)
-        def _():
-            source = k - 2 * step
-            hidden_wait(2 * source + core)
-
-            @pl.when(can_up)
+    def at_distance(step, act):
+        if step == 0:
+            act(k, None)
+        elif 0 < step < length:
+
+            @pl.when(line - step >= 0)
             def _():
-                hidden_copy(source, 0).start()
-
-            hidden_copy(source, 2).start()
-            hidden_copy(source, 3).start()
-
-        @pl.when(line + step < length)
-        def _():
-            source = k + 2 * step
-            hidden_wait(2 * source + core)
-
-            @pl.when(can_down)
+                act(k - 2 * step, (can_up, 0))
+
+            @pl.when(line + step < length)
             def _():
-                hidden_copy(source, 1).start()
-
-            hidden_copy(source, 2).start()
-            hidden_copy(source, 3).start()
-
-        @pl.when(line - step >= 0)
-        def _():
-            across(k - 2 * step + 1 - 2 * side)
-
-        @pl.when(line + step < length)
-        def _():
-            across(k + 2 * step + 1 - 2 * side)
+                act(k + 2 * step, (can_down, 1))
+
+    def along(source, onward):
+        if onward is not None:
+            hidden_wait(source, v)
+            more, where = onward
+
+            @pl.when(more)
+            def _():
+                hidden_copy(source, where).start()
+
+            for where in (2, 3, 4):
+                hidden_copy(source, where).start()
+
+    def across(source, onward):
+        source = source + 1 - 2 * side
+        hidden_wait(source, v)
+        for where in (3, 4):
+            hidden_copy(source, where).start()
+
+    def beside_along(source, onward):
+        if onward is not None:
+            hidden_wait(source, v + 2 - 4 * (v // 2))
+            hidden_copy(source, 5).start()
+
+    def beside_across(source, onward):
+        source = source + 1 - 2 * side
+        hidden_wait(source, v + 2 - 4 * (v // 2))
+        hidden_copy(source, 5).start()
+
+    sent = 0
+    for step in range(length + 2):
+        at_distance(step, along)
+        at_distance(step - 1, across)
+        at_distance(step - 1, beside_along)
+        at_distance(step - 2, beside_across)
+        count = SEND_COUNTS[step] if step < len(SEND_COUNTS) else 0
+        for chunk in range(sent, min(sent + count, len(sends))):
+            send_columns(chunk)
+        sent = min(sent + count, len(sends))
+    for chunk in range(sent, len(sends)):
+        send_columns(chunk)
 
     for copy in own_hidden:
         copy.wait()
 
     @pl.loop(1, nd)
     def _(j):
-        hidden_wait(2 * draw_peer(j) + 1 - core)
+        for part in range(2):
+            hidden_wait(draw_peer(j), 2 * part + 1 - core)
 
     mst[...] = jnp.full_like(mst, LOWEST)
     sst[...] = jnp.zeros_like(sst)
@@ -336,49 +374,64 @@
         def _(j):
             source = draw_peer(j)
 
-            def arrived(piece):
-                _, _, first, count = piece
-                target_ref = w.at[rows_of(source), pl.ds(first, count)]
-                pltpu.make_async_copy(
-                    u_ref.at[:, pl.ds(0, count)], target_ref, urecv.at[chunk, source]
-                ).wait()
-
-            for_target(chunk, k, arrived)
-
-        groups = jnp.clip(limit - start, 0, width) // GROUP
+            for part, (first, count) in enumerate(sends):
+                if start <= first < start + width:
+
+                    def arrived(piece):
+                        target_ref = w.at[rows_of(source), pl.ds(piece[2], piece[3])]
+                        pltpu.make_async_copy(
+                            u_ref.at[:, pl.ds(0, piece[3])], target_ref, urecv.at[part, source]
+                        ).wait()
+
+                    for_target(part, k, arrived)
+
         wt[0:width, :] = w[:, start : start + width].T
 
-        @pl.loop(0, nd)
-        def _(pair):
+        def multiply(pair, x_ref):
             rows = hbuf[pl.ds(2 * pair, 2)].reshape(wide, hbuf.shape[2])
-            xbuf[0:width, :] = lax.dot_general(
+            x_ref[0:width, :] = lax.dot_general(
                 wt[0:width, :], rows, (((1,), (1,)), ((), ())), preferred_element_type=jnp.float32
             )
+
+        def gather(pair, x_ref):
+            if start + width <= full_end:
+                loop, groups = unrolled, width // GROUP
+            else:
+                loop, groups = lax.fori_loop, jnp.clip(limit - start, 0, width) // GROUP
             old = mst[pair]
 
             def largest(group, found):
                 for r in range(GROUP // 8):
-                    at = pl.multiple_of(group * GROUP + r * 8, 8)
-                    found = jnp.maximum(found, xbuf[pl.ds(at, 8), :])
+                    at = group * GROUP + r * 8
+                    found = jnp.maximum(found, x_ref[pl.ds(at, 8), :])
                 return found
 
-            new = lax.fori_loop(0, groups, largest, old)
+            new = loop(0, groups, largest, old)
 
             def totals(group, state):
                 total, chosen = state
                 for r in range(GROUP // 8):
-                    at = pl.multiple_of(group * GROUP + r * 8, 8)
-                    x = xbuf[pl.ds(at, 8), :]
+                    at = group * GROUP + r * 8
+                    x = x_ref[pl.ds(at, 8), :]
                     total = total + jnp.exp(x - new)
-                    chosen = chosen + jnp.where(relative == start + at, x, 0.0)
+                    chosen = jnp.where(relative == start + at, x, chosen)
                 return total, chosen
 
-            total, chosen = lax.fori_loop(
+            total, chosen = loop(
                 0, groups, totals, (sst[pair] * jnp.exp(old - new), cst[pair])
             )
             mst[pair] = new
             sst[pair] = total
             cst[pair] = chosen
+
+        multiply(0, xbuf)
+
+        @pl.loop(0, nd // 2)
+        def _(i):
+            multiply(2 * i + 1, xbuf_other)
+            gather(2 * i, xbuf)
+            multiply(jnp.minimum(2 * i + 2, nd - 1), xbuf)
+            gather(2 * i + 1, xbuf_other)
 
     @pl.loop(0, nd)
     def _(pair):
@@ -475,13 +528,14 @@
     @pl.loop(1, nd)
     def _(j):
         target = draw_peer(j)
-        for chunk in range(len(chunks)):
+        for chunk in range(len(sends)):
             for_target(
                 chunk, target, lambda piece: remote_columns(chunk, target, piece).wait_send()
             )
         stat_copy(target).wait_send()
         loss_copy(target).wait_send()
-        hidden_copy(target, 3).wait_send()
+        for where in (3, 4, 5):
+            hidden_copy(target, where).wait_send()
 
     @pl.loop(1, nv)
     def _(j):
@@ -508,15 +562,18 @@
     depth, column_count = unembed.shape
     share, last_full, _, rest = plan
     chunks = cut(0, last_full, WIDEST) + cut(last_full, share - last_full, NARROW)
+    sends = []
+    for chunk, (start, width) in enumerate(chunks):
+        sends += cut(start // LANES, width // LANES, FINE if chunk < FINE_CHUNKS else WIDEST)
     widest = max(width for _, width in chunks)
-    count = len(chunks)
+    count = len(sends)
     wide = 2 * tokens_each
     tail = jnp.pad(unembed[:, column_count - rest :], ((0, 0), (0, LANES - rest)))
     f32, bf16, dma = jnp.float32, jnp.bfloat16, pltpu.SemaphoreType.DMA
     anywhere = pl.BlockSpec(memory_space=pl.ANY)
     inside = pl.BlockSpec(memory_space=pltpu.VMEM)
     losses = pl.pallas_call(
-        functools.partial(kernel, plan, chunks),
+        functools.partial(kernel, plan, chunks, sends),
         out_shape=jax.ShapeDtypeStruct((nd, wide), f32),
         in_specs=[anywhere, anywhere, anywhere, inside],
         out_specs=inside,
@@ -524,6 +581,7 @@
             pltpu.VMEM((2 * nd, tokens_each, model_width), bf16),
             pltpu.VMEM((model_width, share * LANES), bf16),
             pltpu.VMEM((widest, model_width), bf16),
+            pltpu.VMEM((widest, wide), f32),
             pltpu.VMEM((widest, wide), f32),
             pltpu.VMEM((nd, 8, wide), f32),
             pltpu.VMEM((nd, 8, wide), f32),
@@ -535,8 +593,8 @@
             pltpu.VMEM((8, wide), f32),
             pltpu.VMEM((nd, 8, wide), f32),
             dma((2,)),
+            dma((nd, 6)),
             dma((nd, 4)),
-            dma((2 * nd,)),
             dma((count, nd)),
             dma((count, nd)),
             dma((nd,)),
@@ -547,7 +605,7 @@
             dma((nd,)),
         ],
         compiler_params=pltpu.CompilerParams(
-            collective_id=0, has_side_effects=True, vmem_limit_bytes=48 * 1024 * 1024
+            collective_id=0, has_side_effects=True, vmem_limit_bytes=60 * 1024 * 1024
         ),
     )(hidden, unembed, tail, jnp.tile(targets, 2)[None, :])
     losses = losses.reshape(2 * nd, tokens_each)
@@ -567,9 +625,10 @@
     fits = (
         per_device == 2
         and nd % 2 == 0
-        and nv % 2 == 0
+        and nv == 4
         and depth % 16 == 0
         and tokens_each % LANES == 0
+        and tokens_each % 32 == 0
         and rest > 0
         and rest % GROUP == 0
         and 0 < last_full < share

time: 247 us -> 164 us (0.66)
  Pallas kernels: 241 us -> 160 us
    pallas_call x1, Pallas kernels: 241 us -> 160 us  [fused(): pl.pallas_call(functools.partial(kernel, plan, chunks, sends), out_shape=...]
    unnamed x8 -> x4, local copies, waits for them, and re-layouts: 3.56 us -> 0.59 us
where the time goes in v2:
time: 164 us
  Pallas kernels  160 us (98%)
  local copies, waits for them, and re-layouts  2.71 us (2%)
    pallas_call x1, Pallas kernels, fused(): pl.pallas_call(functools.partial(kernel, plan, chunks, sends), out_shape=...  160 us

profile of v2, /device:TPU:0, one launch (start us, length us, event | category | flops | bytes accessed | tf_op | source)
XLA Modules:
  0.0 164.2 jit_solution(18191153167414781765)
XLA Ops:
  0.0 0.0 copy-start
  0.0 0.8 slice.9
  0.8 0.6 pad.4.tail_ref
  1.4 0.0 copy-done
  1.4 0.6 copy.4
  2.0 160.5 %shard_map.37 = f32[8,768]{1,0:T(8,128)} custom-call(bf16[2,384,896]{2,1,0:T(8,128)(2,1)} %h_ref.1, bf16[112,19008]{1,0:T(8,128)(2,1)} %u_ref.1, bf16[112,128]{1,0:T(8,128)(2,1)} %pad.4.tail_ref, s32[1,768]{1,0:T(1,128)} %bitcast.4), custom_call_target="tpu_custom_call" | custom-call | tf_op jit(solution)/shard_map/pallas_call | solution.py:575
  162.4 0.7 reshape.12
  163.2 0.1 dynamic-slice_reduce_fusion
  163.3 0.9 convolution_multiply_fusion
  (5 shorter events, 0.0 us)
Async XLA Ops:
  0.0 1.4 copy-start
